TPU v7x, 32 devices: a whole 2x2x4 slice. The times are simulated.
32 devices in a mesh: row: 8 (over z, y), col: 4 (over x, core).
Axes of the slice: x: 2, y: 2, z: 4, core: 2. Of those that a mesh axis runs over, the one named last changes fastest.
Arguments:
- blocks: float32 [32, 384, 2048], P(('row', 'col')), may hold values from -1.2 to 1.2
- eps_occ: float32 [32], replicated, may hold values from -3 to -0.3
- eps_vir: float32 [384], replicated, may hold values from 0.1 to 3
- partner: int32 [2, 32], replicated, may hold values from 0 to 31, as said below
Outputs:
- gamma: float32 [32, 384, 2048], P(('row', 'col'))
- density: float32 [384, 384], P('row', 'col')
Inputs may be any that keep to these rules, and one draw needn't show every extreme that they name: Orbital index = row index * 4 + col index. In each round the partner of orbital (r, c) is (sigma_t(r), tau_t(c)), where sigma_t and tau_t are pairings without fixed points of the row indices and of the col indices; so partner[t, partner[t, i]] = i and partner[t, i] != i.
All inputs are finite; a program needn't handle non-finite values.
Results may differ from a plain program's by a relative error of at most 0.0003.
Values sent between devices are 32-bit elements; how exact they have to be, the bound alone decides.
A program may use at most 128 MiB of HBM per device.

v0:
```python
import jax
import jax.numpy as jnp
from jax import lax
from jax.sharding import PartitionSpec as P

ROUNDS = 2


def pair_terms(own_block, mate_block, energy_own, energy_mate, eps_vir):
    pairs = jnp.dot(
        own_block, mate_block.T, precision=lax.Precision.HIGHEST, preferred_element_type=jnp.float32
    )
    denom = eps_vir[:, None] + eps_vir[None, :] - energy_own - energy_mate
    amp = -pairs / denom
    tamp = 2.0 * amp - amp.T
    gamma_term = jnp.dot(
        tamp, mate_block, precision=lax.Precision.HIGHEST, preferred_element_type=jnp.float32
    )
    dens_term = jnp.dot(
        amp, tamp.T, precision=lax.Precision.HIGHEST, preferred_element_type=jnp.float32
    )
    return (gamma_term, dens_term)


def reorder_slabs(block, mapping, axis_dim, count):
    if axis_dim == 0:
        shaped = block.reshape(count, block.shape[0] // count, block.shape[1])
        return jnp.take(shaped, mapping, axis=0).reshape(block.shape)
    shaped = block.reshape(block.shape[0], count, block.shape[1] // count)
    return jnp.take(shaped, mapping, axis=1).reshape(block.shape)


def local(blocks, eps_occ, eps_vir, partner):
    own_block = blocks[0]
    row_count = lax.axis_size("row")
    col_count = lax.axis_size("col")
    row_index = lax.axis_index("row")
    col_index = lax.axis_index("col")
    orbital = row_index * col_count + col_index
    energy_own = lax.dynamic_index_in_dim(eps_occ, orbital, 0, keepdims=False)
    vir_count = own_block.shape[0]
    row_maps = []
    col_maps = []
    energies = []
    for step_index in range(ROUNDS):
        mates = partner[step_index]
        grid = mates.reshape(row_count, col_count)
        row_maps.append(lax.dynamic_index_in_dim(grid, col_index, 1, keepdims=False) // col_count)
        col_maps.append(lax.dynamic_index_in_dim(grid, row_index, 0, keepdims=False) % col_count)
        mate = lax.dynamic_index_in_dim(mates, orbital, 0, keepdims=False)
        energies.append(lax.dynamic_index_in_dim(eps_occ, mate, 0, keepdims=False))
    mate_blocks = []
    for step_index in range(ROUNDS):
        moving = lax.all_to_all(own_block, "row", split_axis=0, concat_axis=0, tiled=True)
        moving = reorder_slabs(moving, row_maps[step_index], 0, row_count)
        moving = lax.all_to_all(moving, "row", split_axis=0, concat_axis=0, tiled=True)
        moving = lax.all_to_all(moving, "col", split_axis=1, concat_axis=1, tiled=True)
        moving = reorder_slabs(moving, col_maps[step_index], 1, col_count)
        mate_blocks.append(lax.all_to_all(moving, "col", split_axis=1, concat_axis=1, tiled=True))
    gamma_sum = jnp.zeros(own_block.shape, jnp.float32)
    dens_sum = jnp.zeros((vir_count, vir_count), jnp.float32)
    for step_index in range(ROUNDS):
        gamma_term, dens_term = pair_terms(
            own_block, mate_blocks[step_index], energy_own, energies[step_index], eps_vir
        )
        gamma_sum = gamma_sum + gamma_term
        dens_sum = dens_sum + dens_term
    partial_rows = lax.psum_scatter(dens_sum, "row", scatter_dimension=0, tiled=True)
    tile = lax.psum_scatter(partial_rows, "col", scatter_dimension=1, tiled=True)
    density = tile / jnp.float32(row_count * col_count)
    return (gamma_sum[None], density)


def solution(mesh):
    in_specs = (P(("row", "col"), None, None), P(), P(), P())
    out_specs = (P(("row", "col"), None, None), P("row", "col"))
    return jax.shard_map(local, mesh=mesh, in_specs=in_specs, out_specs=out_specs, check_vma=False)
```

profile of v0, /device:TPU:0, one launch (start us, length us, event | category | flops | bytes accessed | tf_op | source)
XLA Modules:
  0.0 523.4 jit_solution(3663394454987051395)
XLA Ops:
  7.2 7.3 %all-to-all-start = ((f32[8,48,2048]{2,1,0:T(8,128)}), f32[8,48,2048]{2,1,0:T(8,128)S(1)}, u32[]{:S(2)}, u32[]{:S(2)}) async-start(f32[8,48,2048]{2,1,0:T(8,128)} %bitcast.59), calls=%async_computation | async-start | bytes 6291456 | tf_op jit(solution)/shard_map/all_to_all | solution.py:54
  15.1 70.1 %all-to-all-done = f32[8,48,2048]{2,1,0:T(8,128)S(1)} async-done(((f32[8,48,2048]{2,1,0:T(8,128)}), f32[8,48,2048]{2,1,0:T(8,128)S(1)}, u32[]{:S(2)}, u32[]{:S(2)}) %all-to-all-start) | async-done | bytes 3145760 | tf_op jit(solution)/shard_map/all_to_all | solution.py:54
  87.6 4.0 broadcast_select_fusion.1
  91.6 4.5 all-to-all-start.1
  98.5 4.1 broadcast_select_fusion
  102.6 63.7 %all-to-all-done.1 = f32[8,48,2048]{2,1,0:T(8,128)} async-done(((f32[8,48,2048]{2,1,0:T(8,128)}), f32[8,48,2048]{2,1,0:T(8,128)}, u32[]{:S(2)}, u32[]{:S(2)}) %all-to-all-start.1) | async-done | bytes 3145760 | tf_op jit(solution)/shard_map/all_to_all | solution.py:56
  166.3 3.6 all-to-all-start.4
  169.9 5.2 all_to_all.42
  175.1 4.6 copy.19
  179.7 61.1 %all-to-all-done.4 = f32[8,48,2048]{2,1,0:T(8,128)S(1)} async-done(((f32[8,48,2048]{2,1,0:T(8,128)}), f32[8,48,2048]{2,1,0:T(8,128)S(1)}, u32[]{:S(2)}, u32[]{:S(2)}) %all-to-all-start.4) | async-done | bytes 3145760 | tf_op jit(solution)/shard_map/all_to_all | solution.py:56
  242.5 3.7 all-to-all-start.2
  246.2 5.3 %all_to_all.47 = f32[384,4,512]{2,1,0:T(4,128)} reshape(f32[8,48,2048]{2,1,0:T(8,128)} %copy-done.3) | data formatting | bytes 6291456 | tf_op jit(solution)/shard_map/all_to_all | solution.py:57
  251.5 4.6 copy.22
  256.0 27.0 %all-to-all-done.2 = f32[384,4,512]{2,0,1:T(8,128)S(1)} async-done(((f32[384,4,512]{2,0,1:T(8,128)}), f32[384,4,512]{2,0,1:T(8,128)S(1)}, u32[]{:S(2)}, u32[]{:S(2)}) %all-to-all-start.2) | async-done | bytes 3145760 | tf_op jit(solution)/shard_map/all_to_all | solution.py:57
  284.7 3.7 all-to-all-start.5
  288.5 4.3 gather_fusion.1
  292.8 4.0 select_bitcast_fusion.1
  296.8 28.5 %all-to-all-done.5 = f32[384,4,512]{2,0,1:T(8,128)S(1)} async-done(((f32[384,4,512]{2,0,1:T(8,128)}), f32[384,4,512]{2,0,1:T(8,128)S(1)}, u32[]{:S(2)}, u32[]{:S(2)}) %all-to-all-start.5) | async-done | bytes 3145760 | tf_op jit(solution)/shard_map/all_to_all | solution.py:57
  327.0 3.7 all-to-all-start.3
  330.8 4.3 gather_fusion.3
  335.0 4.0 select_bitcast_fusion
  339.1 28.6 %all-to-all-done.3 = f32[384,4,512]{2,0,1:T(8,128)S(1)} async-done(((f32[384,4,512]{2,0,1:T(8,128)}), f32[384,4,512]{2,0,1:T(8,128)S(1)}, u32[]{:S(2)}, u32[]{:S(2)}) %all-to-all-start.3) | async-done | bytes 3145760 | tf_op jit(solution)/shard_map/all_to_all | solution.py:59
  369.3 4.7 all-to-all-start.6
  381.4 12.6 %fusion.4 = f32[384,384]{1,0:T(8,128)} fusion(f32[384,2048]{0,1:T(8,128)S(1)} %bitcast.57, f32[1,384,2048]{2,1,0:T(8,128)} %param.8), kind=kOutput, calls=%fused_computation.14 | convolution fusion | flops 3624026112 | bytes 6881280 | tf_op jit(solution)/shard_map/dot_general | solution.py:10
  396.2 14.8 %all-to-all-done.6 = f32[384,4,512]{2,0,1:T(8,128)} async-done(((f32[384,4,512]{2,0,1:T(8,128)}), f32[384,4,512]{2,0,1:T(8,128)}, u32[]{:S(2)}, u32[]{:S(2)}) %all-to-all-start.6) | async-done | bytes 3145760 | tf_op jit(solution)/shard_map/all_to_all | solution.py:59
  414.5 8.8 %fusion.7 = f32[384,384]{0,1:T(8,128)} fusion(f32[384,2048]{0,1:T(8,128)} %bitcast.60, f32[1,384,2048]{2,1,0:T(8,128)} %param.8), kind=kOutput, calls=%fused_computation.15 | convolution fusion | flops 3624026112 | bytes 6881280 | tf_op jit(solution)/shard_map/dot_general | solution.py:10
  425.4 4.2 fusion.16
  429.7 3.6 convolution_add_fusion
  433.3 10.9 %fusion.17 = f32[384,2048]{1,0:T(8,128)} fusion(f32[384,2048]{0,1:T(8,128)S(1)} %bitcast.58, f32[384,384]{1,0:T(8,128)} %fusion.4, f32[]{:T(128)} %bitcast.8, f32[]{:T(128)} %bitcast.6, f32[384]{0:T(512)S(1)} %copy-done.6, f32[384,384]{0,1:T(8,128)} %copy.21), kind=kOutput, calls=%fused_computation.63 | convolution fusion | flops 3624910848 | bytes 7472648 | tf_op jit(solution)/shard_map/dot_general | solution.py:16
  444.2 49.4 %reduce-scatter.5.cloned.1.call-done = f32[48,384]{1,0:T(8,128)} async-done(((f32[384,384]{1,0:T(8,128)}), f32[48,384]{1,0:T(8,128)}) %reduce-scatter.5.cloned.1.call-update) | async-done | bytes 73744 | tf_op jit(solution)/shard_map/reduce_scatter | solution.py:68
  495.4 10.2 %add_bitcast_fusion = f32[1,384,2048]{2,1,0:T(8,128)} fusion(f32[384,2048]{1,0:T(8,128)} %fusion.17, f32[384,2048]{0,1:T(8,128)} %bitcast.61, f32[384,384]{1,0:T(8,128)} %copy.25, f32[]{:T(128)} %bitcast.14, f32[]{:T(128)} %bitcast.6, f32[384]{0:T(512)S(1)} %copy-done.6, f32[384,384]{0,1:T(8,128)} %fusion.7), kind=kOutput, calls=%fused_computation.10 | convolution fusion | flops 3625697280 | bytes 10618376 | tf_op jit(solution)/shard_map/dot_general | solution.py:16
  505.6 9.5 %reduce-scatter.7.cloned.1.call-done = f32[96,48]{1,0:T(8,128)} async-done(((f32[384,48]{1,0:T(8,128)}), f32[96,48]{1,0:T(8,128)}) %reduce-scatter.7.cloned.1.call-update) | async-done | bytes 18448
  (45 shorter events, 27.0 us)
Async XLA Ops:
  7.2 7.3 %copy-start.8 = (s32[2,32]{1,0:T(2,128)S(1)}, s32[2,32]{1,0:T(2,128)}, u32[]{:S(2)}) copy-start(s32[2,32]{1,0:T(2,128)} %param.11) | copy-start | bytes 772
  7.2 78.0 %all-to-all-start = ((f32[8,48,2048]{2,1,0:T(8,128)}), f32[8,48,2048]{2,1,0:T(8,128)S(1)}, u32[]{:S(2)}, u32[]{:S(2)}) async-start(f32[8,48,2048]{2,1,0:T(8,128)} %bitcast.59), calls=%async_computation | async-start | bytes 6291456 | tf_op jit(solution)/shard_map/all_to_all | solution.py:54
  91.6 74.6 %all-to-all-start.1 = ((f32[8,48,2048]{2,1,0:T(8,128)}), f32[8,48,2048]{2,1,0:T(8,128)}, u32[]{:S(2)}, u32[]{:S(2)}) async-start(f32[8,48,2048]{2,1,0:T(8,128)} %broadcast_select_fusion.1), calls=%async_computation.1 | async-start | bytes 6291456 | tf_op jit(solution)/shard_map/all_to_all | solution.py:56
  166.3 74.5 %all-to-all-start.4 = ((f32[8,48,2048]{2,1,0:T(8,128)}), f32[8,48,2048]{2,1,0:T(8,128)S(1)}, u32[]{:S(2)}, u32[]{:S(2)}) async-start(f32[8,48,2048]{2,1,0:T(8,128)} %broadcast_select_fusion), calls=%async_computation.4 | async-start | bytes 6291456 | tf_op jit(solution)/shard_map/all_to_all | solution.py:56
  240.8 1.7 copy-start.3
  242.5 40.6 %all-to-all-start.2 = ((f32[384,4,512]{2,0,1:T(8,128)}), f32[384,4,512]{2,0,1:T(8,128)S(1)}, u32[]{:S(2)}, u32[]{:S(2)}) async-start(f32[384,4,512]{2,0,1:T(8,128)} %copy.19), calls=%async_computation.2 | async-start | bytes 6291456 | tf_op jit(solution)/shard_map/all_to_all | solution.py:57
  283.1 1.7 copy-start.2
  284.7 40.6 %all-to-all-start.5 = ((f32[384,4,512]{2,0,1:T(8,128)}), f32[384,4,512]{2,0,1:T(8,128)S(1)}, u32[]{:S(2)}, u32[]{:S(2)}) async-start(f32[384,4,512]{2,0,1:T(8,128)} %copy.22), calls=%async_computation.5 | async-start | bytes 6291456 | tf_op jit(solution)/shard_map/all_to_all | solution.py:57
  325.3 1.7 copy-start.1
  327.0 40.6 %all-to-all-start.3 = ((f32[384,4,512]{2,0,1:T(8,128)}), f32[384,4,512]{2,0,1:T(8,128)S(1)}, u32[]{:S(2)}, u32[]{:S(2)}) async-start(f32[384,4,512]{2,0,1:T(8,128)} %select_bitcast_fusion.1), calls=%async_computation.3 | async-start | bytes 6291456 | tf_op jit(solution)/shard_map/all_to_all | solution.py:59
  339.1 39.3 %copy-start.7 = (f32[32]{0:T(128)S(1)}, f32[32]{0:T(128)}, u32[]{:S(2)}) copy-start(f32[32]{0:T(128)} %param.9) | copy-start | bytes 388
  367.6 1.7 copy-start
  369.3 41.7 %all-to-all-start.6 = ((f32[384,4,512]{2,0,1:T(8,128)}), f32[384,4,512]{2,0,1:T(8,128)}, u32[]{:S(2)}, u32[]{:S(2)}) async-start(f32[384,4,512]{2,0,1:T(8,128)} %select_bitcast_fusion), calls=%async_computation.6 | async-start | bytes 6291456 | tf_op jit(solution)/shard_map/all_to_all | solution.py:59
  373.9 119.7 %reduce-scatter.5.cloned.1.call-start = ((), (), s32[]{:S(2)}) async-start(), calls=%async_computation.9 | async-start | bytes 663552 | tf_op jit(solution)/shard_map/reduce_scatter | solution.py:68
  414.5 10.9 %copy-start.6 = (f32[384]{0:T(512)S(1)}, f32[384]{0:T(512)}, u32[]{:S(2)}) copy-start(f32[384]{0:T(512)} %param.10) | copy-start | bytes 4612
  425.4 4.3 copy-start.4
  425.4 4.3 copy-start.5
  433.3 81.8 %reduce-scatter.7.cloned.1.call-start = ((), (), s32[]{:S(2)}) async-start(), calls=%async_computation.10 | async-start | bytes 245760
Sparse Core Ops, SparseCore 0:
  433.4 60.2 reduce-scatter.4
  496.3 18.7 reduce-scatter.6
where the time goes:
time: 525 us; the launch traced here: 523 us
  waiting for transfers between devices  353 us (67%)
  local copies, waits for them, and re-layouts  54.3 us (10%)
  matrix products  50.4 us (10%)
  starting transfers between devices  31.4 us (6%)
  between operations  17.8 us (3%)
  other arithmetic  16.8 us (3%)
    all_to_all x2, waiting for transfers between devices, local(): lax.all_to_all(moving, 'row', split_axis=0, concat_axis=0, tiled=True)  125 us
    all_to_all x4, waiting for transfers between devices, local(): lax.all_to_all(moving, 'col', split_axis=1, concat_axis=1, tiled=True)  98.9 us
    all_to_all x1, waiting for transfers between devices, local(): lax.all_to_all(own_block, 'row', split_axis=0, concat_axis=0, tiled=True)  70.1 us
    reduce_scatter x1, waiting for transfers between devices, local(): lax.psum_scatter(dens_sum, 'row', scatter_dimension=0, tiled=True)  49.4 us
    all_to_all x6, local copies, waits for them, and re-layouts, local(): lax.all_to_all(moving, 'col', split_axis=1, concat_axis=1, tiled=True)  25.6 us
    dot_general x2, matrix products, pair_terms(): jnp.dot(own_block, mate_block.T, precision=lax.Precision.HIGHEST, preferr...  21.4 us
    dot_general x2, matrix products, pair_terms(): jnp.dot(tamp, mate_block, precision=lax.Precision.HIGHEST, preferred_elem...  21.1 us
    all_to_all x4, starting transfers between devices, local(): lax.all_to_all(moving, 'col', split_axis=1, concat_axis=1, tiled=True)  15.8 us
  transfers between devices with their start and end apart: 9, of which 9 were waited for; matrix products, arithmetic and copies ran while one was open for 14% of the time, Pallas kernels for 0%

commit v1 on v0

v1 whole, which is shorter than its diff:
```python
import functools

import jax
import jax.numpy as jnp
from jax import lax
from jax.experimental import pallas as pl
from jax.experimental.pallas import tpu as pltpu
from jax.sharding import PartitionSpec as P

MESH = pl.DeviceIdType.MESH
CHUNKS = 8
DOT = lax.Precision.HIGH


def exchange_kernel(n_row, n_col, rounds, chunks, partner_ref, own_ref, mate_ref, *scratch):
    lines, sels, fwds = scratch[:chunks], scratch[chunks : 2 * chunks], scratch[2 * chunks : 3 * chunks]
    s1s, s1r, s2s, s2r, s3s, s3r, s4s, s4r, local1, local4 = scratch[3 * chunks :]
    nz, plane = n_row // 2, 2 * n_col
    half = nz // 2
    deep = own_ref.shape[0] // 2
    rows, width = deep // chunks, own_ref.shape[1] // n_col
    row, col = lax.axis_index("row"), lax.axis_index("col")
    z, y = row // 2, row % 2
    p = y * n_col + col
    upper = z // half
    hub_near = half - 1 + upper
    hub_far = half - upper
    is_hub = z == hub_near

    def device(zz, q):
        return (zz * 2 + q // n_col, q % n_col)

    def piece(q, k):
        return (
            pl.ds(pl.multiple_of(q // n_col * deep + k * rows, 8), rows),
            pl.ds(pl.multiple_of(q % n_col * width, 128), width),
        )

    def block(zz):
        return pl.ds(zz * plane, plane)

    def spread(k, o):
        q = lax.rem(p + o, plane)
        return pltpu.make_async_remote_copy(
            src_ref=own_ref.at[piece(q, k)],
            dst_ref=lines[k].at[z * plane + p],
            send_sem=s1s.at[k, o],
            recv_sem=s1r.at[k, o],
            device_id=device(z, q),
            device_id_type=MESH,
        )

    def spread_own(k):
        return pltpu.make_async_copy(own_ref.at[piece(p, k)], lines[k].at[z * plane + p], local1.at[k])

    def to_hub(k, slot, hub):
        return pltpu.make_async_remote_copy(
            src_ref=lines[k].at[block(z)],
            dst_ref=lines[k].at[block(z)],
            send_sem=s2s.at[k, slot],
            recv_sem=s2r.at[k, z],
            device_id=device(hub, p),
            device_id_type=MESH,
        )

    def from_z(k, zz):
        return pltpu.make_async_remote_copy(
            src_ref=lines[k].at[block(zz)],
            dst_ref=lines[k].at[block(zz)],
            send_sem=s2s.at[k, 0],
            recv_sem=s2r.at[k, zz],
            device_id=device(hub_far, p),
            device_id_type=MESH,
        )

    def served(i):
        return (1 - upper) * (half - 2 - i) + upper * (half + 1 + i)

    def serve(k, i, zz):
        return pltpu.make_async_remote_copy(
            src_ref=fwds[k].at[i],
            dst_ref=sels[k],
            send_sem=s3s.at[k, i],
            recv_sem=s3r.at[k],
            device_id=device(zz, p),
            device_id_type=MESH,
        )

    def back(k, t, o):
        q = lax.rem(p + o, plane)
        return pltpu.make_async_remote_copy(
            src_ref=sels[k].at[t * plane + q],
            dst_ref=mate_ref.at[(t,) + piece(p, k)],
            send_sem=s4s.at[k, t, o],
            recv_sem=s4r.at[k, t, o],
            device_id=device(z, q),
            device_id_type=MESH,
        )

    def back_own(k, t):
        return pltpu.make_async_copy(
            sels[k].at[t * plane + p], mate_ref.at[(t,) + piece(p, k)], local4.at[k, t]
        )

    def each(count, start, body):
        def step(i, carry):
            body(i)
            return carry

        lax.fori_loop(start, count, step, 0)

    barrier = pltpu.get_barrier_semaphore()

    def greet_plane(o):
        pl.semaphore_signal(barrier, inc=1, device_id=device(z, lax.rem(p + o, plane)), device_id_type=MESH)

    def greet_line(o):
        pl.semaphore_signal(barrier, inc=1, device_id=device(lax.rem(z + o, nz), p), device_id_type=MESH)

    each(plane, 1, greet_plane)
    each(nz, 1, greet_line)
    pl.semaphore_wait(barrier, plane - 1 + nz - 1)

    def start_spread(k):
        spread_own(k).start()
        each(plane, 1, lambda o: spread(k, o).start())

    def send_line(k):
        spread_own(k).wait()
        each(plane, 1, lambda o: spread(k, o).wait_recv())
        to_hub(k, 0, hub_far).start()

        @pl.when(jnp.logical_not(is_hub))
        def _():
            to_hub(k, 1, hub_near).start()

    def send_back(k):
        for t in range(rounds):
            back_own(k, t).start()
            each(plane, 1, lambda o: back(k, t, o).start())

    def hub_step(k):
        each(nz, 1, lambda o: from_z(k, lax.rem(z + o, nz)).wait_recv())
        for i in range(half - 1):
            zz = served(i)

            def pick_far(j):
                want = partner_ref[j // plane, zz * plane + lax.rem(j, plane)]
                fwds[k][i, j] = lines[k][want]

            each(rounds * plane, 0, pick_far)
            serve(k, i, zz).start()

        def pick_own(j):
            want = partner_ref[j // plane, z * plane + lax.rem(j, plane)]
            sels[k][j] = lines[k][want]

        each(rounds * plane, 0, pick_own)
        send_back(k)

    def leaf_step(k):
        serve(k, 0, hub_near).wait_recv()
        send_back(k)

    start_spread(0)
    for s in range(chunks + 2):
        if s + 1 < chunks:
            start_spread(s + 1)
        if s < chunks:
            send_line(s)
        if 1 <= s <= chunks:
            pl.when(is_hub)(functools.partial(hub_step, s - 1))
        if s >= 2:
            pl.when(jnp.logical_not(is_hub))(functools.partial(leaf_step, s - 2))

    for k in range(chunks):
        for t in range(rounds):
            back_own(k, t).wait()
            each(plane, 1, lambda o: back(k, t, o).wait())
        each(plane, 1, lambda o: spread(k, o).wait_send())
        to_hub(k, 0, hub_far).wait_send()

        @pl.when(jnp.logical_not(is_hub))
        def _():
            to_hub(k, 1, hub_near).wait_send()

        @pl.when(is_hub)
        def _():
            for i in range(half - 1):
                serve(k, i, served(i)).wait_send()


def exchange(n_row, n_col, partner, own):
    rounds = partner.shape[0]
    nz, plane = n_row // 2, 2 * n_col
    leaves = nz // 2 - 1
    chunks = CHUNKS
    rows, width = own.shape[0] // 2 // chunks, own.shape[1] // n_col
    piece = (rows, width)
    dma = pltpu.SemaphoreType.DMA
    held = (nz + rounds * (leaves + 1)) * plane * rows * width * 4 * chunks
    return pl.pallas_call(
        functools.partial(exchange_kernel, n_row, n_col, rounds, chunks),
        out_shape=jax.ShapeDtypeStruct((rounds,) + own.shape, jnp.float32),
        in_specs=[pl.BlockSpec(memory_space=pltpu.SMEM), pl.BlockSpec(memory_space=pl.ANY)],
        out_specs=pl.BlockSpec(memory_space=pl.ANY),
        scratch_shapes=[pltpu.VMEM((nz * plane,) + piece, jnp.float32)] * chunks
        + [pltpu.VMEM((rounds * plane,) + piece, jnp.float32)] * chunks
        + [pltpu.VMEM((leaves, rounds * plane) + piece, jnp.float32)] * chunks
        + [
            dma((chunks, plane)),
            dma((chunks, plane)),
            dma((chunks, 2)),
            dma((chunks, nz)),
            dma((chunks, leaves)),
            dma((chunks,)),
            dma((chunks, rounds, plane)),
            dma((chunks, rounds, plane)),
            dma((chunks,)),
            dma((chunks, rounds)),
        ],
        compiler_params=pltpu.CompilerParams(
            collective_id=0, has_side_effects=True, vmem_limit_bytes=held + 4 * 2**20
        ),
        name="exchange",
    )(partner, own)


def local(blocks, eps_occ, eps_vir, partner):
    own = blocks[0]
    n_row, n_col = lax.axis_size("row"), lax.axis_size("col")
    orbital = lax.axis_index("row") * n_col + lax.axis_index("col")
    energy_own = lax.dynamic_index_in_dim(eps_occ, orbital, 0, keepdims=False)
    mates = exchange(n_row, n_col, partner, own)
    rounds = partner.shape[0]
    tamps = []
    dens = 0.0
    for t in range(rounds):
        mate = lax.dynamic_index_in_dim(partner[t], orbital, 0, keepdims=False)
        energy = lax.dynamic_index_in_dim(eps_occ, mate, 0, keepdims=False)
        pairs = jnp.dot(own, mates[t].T, precision=DOT, preferred_element_type=jnp.float32)
        denom = eps_vir[:, None] + eps_vir[None, :] - energy_own - energy
        amp = -pairs / denom
        tamp = 2.0 * amp - amp.T
        tamps.append(tamp)
        dens = dens + jnp.dot(amp, tamp.T, precision=DOT, preferred_element_type=jnp.float32)
    part = lax.psum_scatter(dens, "row", scatter_dimension=0, tiled=True)
    tile = lax.psum_scatter(part, "col", scatter_dimension=1, tiled=True)
    gamma = 0.0
    for t in range(rounds):
        gamma = gamma + jnp.dot(tamps[t], mates[t], precision=DOT, preferred_element_type=jnp.float32)
    return gamma[None], tile / jnp.float32(n_row * n_col)


def solution(mesh):
    in_specs = (P(("row", "col"), None, None), P(), P(), P())
    out_specs = (P(("row", "col"), None, None), P("row", "col"))
    return jax.shard_map(local, mesh=mesh, in_specs=in_specs, out_specs=out_specs, check_vma=False)
```

time: 525 us -> 301 us (0.57)
  waiting for transfers between devices: 353 us -> 65.7 us
  Pallas kernels: 0 us -> 183 us
  local copies, waits for them, and re-layouts: 54.3 us -> 7.67 us
  starting transfers between devices: 31.4 us -> 0.26 us
  matrix products: 50.4 us -> 24.6 us
  other arithmetic: 16.8 us -> 0.63 us
    all_to_all x7 -> x0, waiting for transfers between devices: 294 us -> none  [the longest x2 125 us: local(): lax.all_to_all(moving, 'row', split_axis=0, concat_axis=0, tiled=True)]
    pallas_call x0 -> x1, Pallas kernels: none -> 183 us  [exchange(): pl.pallas_call(functools.partial(exchange_kernel, n_row, n_col, rounds, c...]
    all_to_all x7 -> x0, starting transfers between devices: 31.2 us -> none  [the longest x4 15.8 us: local(): lax.all_to_all(moving, 'col', split_axis=1, concat_axis=1, tiled=True)]
    dot_general x6, matrix products: 50.4 us -> 24.6 us  [the longest x2 14.2 us: local(): jnp.dot(tamps[t], mates[t], precision=DOT, preferred_element_type=jnp.flo...]
    all_to_all x6 -> x0, local copies, waits for them, and re-layouts: 25.6 us -> none  [local(): lax.all_to_all(moving, 'col', split_axis=1, concat_axis=1, tiled=True)]
    select_n x4 -> x0, other arithmetic: 16.1 us -> none  [the longest x2 8.09 us: reorder_slabs(): return jnp.take(shaped, mapping, axis=0).reshape(block.shape)]
    gather x4 -> x0, local copies, waits for them, and re-layouts: 13.4 us -> none  [the longest x2 8.57 us: reorder_slabs(): return jnp.take(shaped, mapping, axis=1).reshape(block.shape)]
  transfers between devices with their start and end apart: 9 -> 2, of which waited for: 9 -> 2; matrix products, arithmetic and copies ran while one was open for 14% -> 5% of each run, Pallas kernels for 0% -> 0%
where the time goes in v1:
time: 301 us; the launch traced here: 300 us
  Pallas kernels  183 us (61%)
  waiting for transfers between devices  65.7 us (22%)
  matrix products  24.6 us (8%)
  between operations  18.2 us (6%)
  local copies, waits for them, and re-layouts  7.67 us (3%)
    pallas_call x1, Pallas kernels, exchange(): pl.pallas_call(functools.partial(exchange_kernel, n_row, n_col, rounds, c...  183 us
    reduce_scatter x1, waiting for transfers between devices, local(): part = lax.psum_scatter(dens, 'row', scatter_dimension=0, tiled=True)  54 us
    dot_general x2, matrix products, local(): jnp.dot(tamps[t], mates[t], precision=DOT, preferred_element_type=jnp.flo...  14.2 us
    unnamed x3, waiting for transfers between devices  11.8 us
  transfers between devices with their start and end apart: 2, of which 2 were waited for; matrix products, arithmetic and copies ran while one was open for 5% of the time, Pallas kernels for 0%

profile of v1, /device:TPU:0, one launch (start us, length us, event | category | flops | bytes accessed | tf_op | source)
XLA Modules:
  0.0 300.4 jit_solution(13657160106526529623)
XLA Ops:
  7.2 0.0 reduce-scatter.5.cloned.1.call-start
  7.2 0.8 fusion.25
  8.0 0.7 constant_dynamic-slice_fusion
  11.3 0.0 copy-start.1
  11.3 1.9 copy-done.1
  13.2 0.7 copy-done.2
  13.9 183.3 %exchange.1 = f32[2,384,2048]{2,1,0:T(8,128)S(1)} custom-call(s32[2,32]{1,0:T(2,128)S(1)} %copy-done.2, f32[384,2048]{1,0:T(8,128)S(1)} %bitcast.44), custom_call_target="tpu_custom_call" | custom-call | tf_op jit(solution)/shard_map/exchange/pallas_call | solution.py:202
  197.2 0.0 copy-start
  197.2 2.6 fusion.17
  199.8 0.0 copy-done
  199.9 2.6 fusion.14
  202.5 0.0 copy-start.3
  202.5 0.2 copy.11
  202.7 0.0 copy-start.6
  202.7 0.2 copy.9
  203.0 0.0 copy-start.5
  204.3 0.0 copy-done.8
  204.3 0.6 fusion.26
  205.0 0.0 copy-done.7
  205.0 2.2 fusion.24
  207.1 0.0 copy-done.3
  207.2 3.0 %convolution_add_fusion = f32[384,384]{1,0:T(8,128)} fusion(f32[384,384]{1,0:T(8,128)S(1)} %fusion.24, f32[384,384]{0,1:T(8,128)S(1)} %fusion.17, f32[]{:T(128)} %bitcast.9, f32[]{:T(128)} %bitcast.3, f32[384]{0:T(512)S(1)} %copy-done.7, f32[384,384]{1,0:T(8,128)S(1)} %copy.11), kind=kOutput, calls=%fused_computation.13 | convolution fusion | flops 341508096 | bytes 2360840 | tf_op jit(solution)/shard_map/dot_general | solution.py:246
  210.2 0.0 reduce-scatter.5.cloned.1.call-update
  210.2 0.2 reduce-scatter.7.cloned.1.call-start
  210.5 6.3 %fusion = f32[384,2048]{1,0:T(8,128)S(1)} fusion(f32[2,384,2048]{2,1,0:T(8,128)} %copy-done, f32[384,384]{1,0:T(8,128)} %copy-done.6, f32[]{:T(128)} %bitcast.9, f32[]{:T(128)} %bitcast.3, f32[384]{0:T(512)S(1)} %copy-done.7, f32[384,384]{0,1:T(8,128)} %copy-done.4), kind=kOutput, calls=%fused_computation | convolution fusion | flops 1812971520 | bytes 7476224 | tf_op jit(solution)/shard_map/dot_general | solution.py:251
  216.7 54.0 %reduce-scatter.5.cloned.1.call-done = f32[48,384]{1,0:T(8,128)} async-done(((f32[384,384]{1,0:T(8,128)}), f32[48,384]{1,0:T(8,128)}) %reduce-scatter.5.cloned.1.call-update) | async-done | bytes 73744 | tf_op jit(solution)/shard_map/reduce_scatter | solution.py:247
  270.7 1.7 copy.13
  272.4 0.0 reduce-scatter.7.cloned.1.call-update
  272.4 7.9 %add_bitcast_fusion = f32[1,384,2048]{2,1,0:T(8,128)} fusion(f32[384,2048]{1,0:T(8,128)S(1)} %fusion, f32[2,384,2048]{2,1,0:T(8,128)} %copy-done, f32[384,384]{1,0:T(8,128)} %copy-done.3, f32[]{:T(128)} %bitcast.5, f32[]{:T(128)} %bitcast.3, f32[384]{0:T(512)S(1)} %copy-done.7, f32[384,384]{0,1:T(8,128)} %copy-done.5), kind=kOutput, calls=%fused_computation.8 | convolution fusion | flops 1813757952 | bytes 10621952 | tf_op jit(solution)/shard_map/dot_general | solution.py:251
  280.3 11.7 %reduce-scatter.7.cloned.1.call-done = f32[96,48]{1,0:T(8,128)} async-done(((f32[384,48]{1,0:T(8,128)}), f32[96,48]{1,0:T(8,128)}) %reduce-scatter.7.cloned.1.call-update) | async-done | bytes 18448
  292.0 0.9 copy.14
  292.9 0.6 broadcast_multiply_fusion
  (7 shorter events, 0.0 us)
Async XLA Ops:
  7.2 263.5 %reduce-scatter.5.cloned.1.call-start = ((), (), s32[]{:S(2)}) async-start(), calls=%async_computation.2 | async-start | bytes 663552 | tf_op jit(solution)/shard_map/reduce_scatter | solution.py:247
  11.3 1.9 copy-start.1
  13.2 0.7 copy-start.2
  197.2 2.7 copy-start
  199.9 7.3 %copy-start.4 = (f32[384,384]{0,1:T(8,128)}, f32[384,384]{0,1:T(8,128)S(1)}, u32[]{:S(2)}) copy-start(f32[384,384]{0,1:T(8,128)S(1)} %fusion.17) | copy-start | bytes 1769476
  199.9 4.5 %copy-start.8 = (f32[32]{0:T(128)S(1)}, f32[32]{0:T(128)}, u32[]{:S(2)}) copy-start(f32[32]{0:T(128)} %param.5) | copy-start | bytes 388
  199.9 5.1 %copy-start.7 = (f32[384]{0:T(512)S(1)}, f32[384]{0:T(512)}, u32[]{:S(2)}) copy-start(f32[384]{0:T(512)} %param.6) | copy-start | bytes 4612
  202.5 4.6 %copy-start.3 = (f32[384,384]{1,0:T(8,128)}, f32[384,384]{1,0:T(8,128)S(1)}, u32[]{:S(2)}) copy-start(f32[384,384]{1,0:T(8,128)S(1)} %fusion.14) | copy-start | bytes 1769476
  202.7 4.4 %copy-start.6 = (f32[384,384]{1,0:T(8,128)}, f32[384,384]{1,0:T(8,128)S(1)}, u32[]{:S(2)}) copy-start(f32[384,384]{1,0:T(8,128)S(1)} %copy.11) | copy-start | bytes 1769476
  203.0 4.2 %copy-start.5 = (f32[384,384]{0,1:T(8,128)}, f32[384,384]{0,1:T(8,128)S(1)}, u32[]{:S(2)}) copy-start(f32[384,384]{0,1:T(8,128)S(1)} %copy.9) | copy-start | bytes 1769476
  210.2 81.8 %reduce-scatter.7.cloned.1.call-start = ((), (), s32[]{:S(2)}) async-start(), calls=%async_computation.3 | async-start | bytes 245760
Sparse Core Ops, SparseCore 0:
  210.3 60.2 reduce-scatter.4
  273.3 18.7 reduce-scatter.6

commit v2 on v1

--- a/solution.py
+++ b/solution.py
@@ -8,7 +8,7 @@
 from jax.sharding import PartitionSpec as P
 
 MESH = pl.DeviceIdType.MESH
-CHUNKS = 8
+CHUNKS = 12
 DOT = lax.Precision.HIGH
 
 
@@ -226,6 +226,102 @@
     )(partner, own)
 
 
+def reduce_kernel(n_row, n_col, own_ref, out_ref, landed, total, final, as_, ar, bs, br):
+    nz, plane = n_row // 2, 2 * n_col
+    row, col = lax.axis_index("row"), lax.axis_index("col")
+    z, y = row // 2, row % 2
+    p = y * n_col + col
+
+    def device(zz, q):
+        return (zz * 2 + q // n_col, q % n_col)
+
+    def each(count, body):
+        def step(i, carry):
+            body(i)
+            return carry
+
+        lax.fori_loop(1, count, step, 0)
+
+    def in_plane(o):
+        q = lax.rem(p + o, plane)
+        return pltpu.make_async_remote_copy(
+            src_ref=own_ref.at[q],
+            dst_ref=landed.at[o],
+            send_sem=as_.at[o],
+            recv_sem=ar.at[o],
+            device_id=device(z, q),
+            device_id_type=MESH,
+        )
+
+    def in_line(o):
+        zz = lax.rem(z + o, nz)
+        return pltpu.make_async_remote_copy(
+            src_ref=total.at[zz],
+            dst_ref=final.at[o],
+            send_sem=bs.at[o],
+            recv_sem=br.at[o],
+            device_id=device(zz, p),
+            device_id_type=MESH,
+        )
+
+    barrier = pltpu.get_barrier_semaphore()
+
+    def greet_plane(o):
+        pl.semaphore_signal(barrier, inc=1, device_id=device(z, lax.rem(p + o, plane)), device_id_type=MESH)
+
+    def greet_line(o):
+        pl.semaphore_signal(barrier, inc=1, device_id=device(lax.rem(z + o, nz), p), device_id_type=MESH)
+
+    each(plane, greet_plane)
+    each(nz, greet_line)
+    pl.semaphore_wait(barrier, plane - 1 + nz - 1)
+    each(plane, lambda o: in_plane(o).start())
+    total[...] = own_ref[p]
+
+    def add_plane(o):
+        in_plane(o).wait_recv()
+        total[...] += landed[o]
+
+    each(plane, add_plane)
+    each(nz, lambda o: in_line(o).start())
+    final[0] = total[z]
+
+    def add_line(o):
+        in_line(o).wait_recv()
+        final[0] += final[o]
+
+    each(nz, add_line)
+    out_ref[...] = final[0] / (n_row * n_col)
+    each(plane, lambda o: in_plane(o).wait_send())
+    each(nz, lambda o: in_line(o).wait_send())
+
+
+def reduce_density(n_row, n_col, dens):
+    nz, plane = n_row // 2, 2 * n_col
+    tile = (dens.shape[0] // n_row, dens.shape[1] // n_col)
+    pieces = dens.reshape(nz, 2, tile[0], n_col, tile[1]).transpose(1, 3, 0, 2, 4).reshape((plane, nz) + tile)
+    dma = pltpu.SemaphoreType.DMA
+    return pl.pallas_call(
+        functools.partial(reduce_kernel, n_row, n_col),
+        out_shape=jax.ShapeDtypeStruct(tile, jnp.float32),
+        in_specs=[pl.BlockSpec(memory_space=pltpu.VMEM)],
+        out_specs=pl.BlockSpec(memory_space=pltpu.VMEM),
+        scratch_shapes=[
+            pltpu.VMEM((plane, nz) + tile, jnp.float32),
+            pltpu.VMEM((nz,) + tile, jnp.float32),
+            pltpu.VMEM((nz,) + tile, jnp.float32),
+            dma((plane,)),
+            dma((plane,)),
+            dma((nz,)),
+            dma((nz,)),
+        ],
+        compiler_params=pltpu.CompilerParams(
+            collective_id=1, has_side_effects=True, vmem_limit_bytes=16 * 2**20
+        ),
+        name="reduce_density",
+    )(pieces)
+
+
 def local(blocks, eps_occ, eps_vir, partner):
     own = blocks[0]
     n_row, n_col = lax.axis_size("row"), lax.axis_size("col")
@@ -233,23 +329,22 @@
     energy_own = lax.dynamic_index_in_dim(eps_occ, orbital, 0, keepdims=False)
     mates = exchange(n_row, n_col, partner, own)
     rounds = partner.shape[0]
-    tamps = []
-    dens = 0.0
+    vir = own.shape[0]
+    stacked = mates.reshape(rounds * vir, own.shape[1])
+    pairs = jnp.dot(own, stacked.T, precision=DOT, preferred_element_type=jnp.float32)
+    amps, tamps = [], []
     for t in range(rounds):
         mate = lax.dynamic_index_in_dim(partner[t], orbital, 0, keepdims=False)
         energy = lax.dynamic_index_in_dim(eps_occ, mate, 0, keepdims=False)
-        pairs = jnp.dot(own, mates[t].T, precision=DOT, preferred_element_type=jnp.float32)
         denom = eps_vir[:, None] + eps_vir[None, :] - energy_own - energy
-        amp = -pairs / denom
-        tamp = 2.0 * amp - amp.T
-        tamps.append(tamp)
-        dens = dens + jnp.dot(amp, tamp.T, precision=DOT, preferred_element_type=jnp.float32)
-    part = lax.psum_scatter(dens, "row", scatter_dimension=0, tiled=True)
-    tile = lax.psum_scatter(part, "col", scatter_dimension=1, tiled=True)
-    gamma = 0.0
-    for t in range(rounds):
-        gamma = gamma + jnp.dot(tamps[t], mates[t], precision=DOT, preferred_element_type=jnp.float32)
-    return gamma[None], tile / jnp.float32(n_row * n_col)
+        amp = -pairs[:, t * vir : (t + 1) * vir] / denom
+        amps.append(amp)
+        tamps.append(2.0 * amp - amp.T)
+    amps, tamps = jnp.concatenate(amps, axis=1), jnp.concatenate(tamps, axis=1)
+    dens = jnp.dot(amps, tamps.T, precision=DOT, preferred_element_type=jnp.float32)
+    tile = reduce_density(n_row, n_col, dens)
+    gamma = jnp.dot(tamps, stacked, precision=DOT, preferred_element_type=jnp.float32)
+    return gamma[None], tile
 
 
 def solution(mesh):

time: 301 us -> 222 us (0.74)
  waiting for transfers between devices: 65.7 us -> 0 us
  between operations: 18.2 us -> 4.62 us
  Pallas kernels: 183 us -> 192 us
  matrix products: 24.6 us -> 15.7 us
    reduce_scatter x1 -> x0, waiting for transfers between devices: 54 us -> none  [local(): part = lax.psum_scatter(dens, 'row', scatter_dimension=0, tiled=True)]
    pallas_call x0 -> x1, Pallas kernels: none -> 16.5 us  [reduce_density(): pl.pallas_call(functools.partial(reduce_kernel, n_row, n_col), out_shape=...]
    unnamed x3 -> x0, waiting for transfers between devices: 11.8 us -> none
    dot_general x6 -> x3, matrix products: 24.6 us -> 15.7 us  [the longest x1 8.6 us: local(): jnp.dot(tamps, stacked, precision=DOT, preferred_element_type=jnp.float32)]
    pallas_call x1, Pallas kernels: 183 us -> 175 us  [exchange(): pl.pallas_call(functools.partial(exchange_kernel, n_row, n_col, rounds, c...]
  transfers between devices with their start and end apart: 2 -> 0, of which waited for: 2 -> 0; matrix products, arithmetic and copies ran while one was open for 5% -> 0% of each run, Pallas kernels for 0% -> 0%
where the time goes in v2:
time: 222 us; the launch traced here: 221 us
  Pallas kernels  192 us (86%)
  matrix products  15.7 us (7%)
  local copies, waits for them, and re-layouts  6.88 us (3%)
  between operations  4.62 us (2%)
  other arithmetic  2.22 us (1%)
    pallas_call x1, Pallas kernels, exchange(): pl.pallas_call(functools.partial(exchange_kernel, n_row, n_col, rounds, c...  175 us
    pallas_call x1, Pallas kernels, reduce_density(): pl.pallas_call(functools.partial(reduce_kernel, n_row, n_col), out_shape=...  16.5 us
    dot_general x1, matrix products, local(): jnp.dot(tamps, stacked, precision=DOT, preferred_element_type=jnp.float32)  8.6 us
    dot_general x1, matrix products, local(): jnp.dot(own, stacked.T, precision=DOT, preferred_element_type=jnp.float32)  5.04 us

profile of v2, /device:TPU:0, one launch (start us, length us, event | category | flops | bytes accessed | tf_op | source)
XLA Modules:
  0.0 221.3 jit_solution(18211166078282610037)
XLA Ops:
  0.6 0.8 fusion.9
  1.4 0.6 constant_dynamic-slice_fusion
  5.9 1.4 fusion.10
  7.2 0.0 copy-start.1
  7.2 1.9 copy-done.1
  9.1 0.0 copy-start.2
  9.1 0.7 copy-done.2
  9.8 175.4 %exchange.1 = f32[2,384,2048]{2,1,0:T(8,128)S(1)} custom-call(s32[2,32]{1,0:T(2,128)S(1)} %copy-done.2, f32[384,2048]{1,0:T(8,128)S(1)} %bitcast.24), custom_call_target="tpu_custom_call" | custom-call | tf_op jit(solution)/shard_map/exchange/pallas_call | solution.py:202
  185.2 0.0 copy-start
  185.3 0.0 copy-start.3
  185.3 5.0 %convolution_bitcast_fusion.1 = f32[384,768]{0,1:T(8,128)S(1)} fusion(f32[768,2048]{1,0:T(8,128)S(1)} %bitcast.22, f32[1,384,2048]{2,1,0:T(8,128)S(1)} %copy-done.1), kind=kOutput, calls=%fused_computation.1 | convolution fusion | flops 3623878656 | bytes 10616832 | tf_op jit(solution)/shard_map/dot_general | solution.py:334
  190.3 0.0 copy-done
  190.3 0.0 copy-done.3
  190.3 2.1 fusion.5
  192.4 0.2 copy.6
  192.7 0.1 bitcast_subtract_fusion.1
  192.7 0.2 copy.7
  193.0 0.1 bitcast_subtract_fusion
  193.0 2.0 fusion
  195.1 0.5 reshape.20
  195.5 0.1 copy.8
  195.6 16.5 %reduce_density.1 = f32[48,96]{1,0:T(8,128)S(1)} custom-call(f32[8,4,48,96]{3,2,1,0:T(8,128)S(1)} %bitcast.25), custom_call_target="tpu_custom_call" | custom-call | tf_op jit(solution)/shard_map/reduce_density/pallas_call | solution.py:304
  212.1 8.6 %convolution_bitcast_fusion = f32[1,384,2048]{2,1,0:T(8,128)} fusion(f32[768,2048]{1,0:T(8,128)} %bitcast.23, f32[384,384]{1,0:T(8,128)S(1)} %bitcast_subtract_fusion, f32[384,384]{1,0:T(8,128)S(1)} %bitcast_subtract_fusion.1), kind=kOutput, calls=%fused_computation | convolution fusion | flops 3624173568 | bytes 10616832 | tf_op jit(solution)/shard_map/dot_general | solution.py:346
  220.7 0.6 copy.10
Async XLA Ops:
  7.2 1.9 copy-start.1
  9.1 0.7 copy-start.2
  185.2 5.1 %copy-start = (f32[2,384,2048]{2,1,0:T(8,128)}, f32[2,384,2048]{2,1,0:T(8,128)S(1)}, u32[]{:S(2)}) copy-start(f32[2,384,2048]{2,1,0:T(8,128)S(1)} %exchange.1) | copy-start | bytes 18874372
  185.3 5.1 %copy-start.3 = (f32[384]{0:T(512)S(1)}, f32[384]{0:T(512)}, u32[]{:S(2)}) copy-start(f32[384]{0:T(512)} %param.6) | copy-start | bytes 4612

commit v3 on v2

--- a/solution.py
+++ b/solution.py
@@ -8,11 +8,14 @@
 from jax.sharding import PartitionSpec as P
 
 MESH = pl.DeviceIdType.MESH
-CHUNKS = 12
+CHUNKS = 24
+SEMAPHORES = 2400
+AHEAD, HUB_LAG, LEAF_LAG = 1, 1, 2
+COLUMNS = 256
 DOT = lax.Precision.HIGH
 
 
-def exchange_kernel(n_row, n_col, rounds, chunks, partner_ref, own_ref, mate_ref, *scratch):
+def exchange_kernel(n_row, n_col, rounds, chunks, partner_ref, eps_ref, own_ref, mate_ref, energy_ref, *scratch):
     lines, sels, fwds = scratch[:chunks], scratch[chunks : 2 * chunks], scratch[2 * chunks : 3 * chunks]
     s1s, s1r, s2s, s2r, s3s, s3r, s4s, s4r, local1, local4 = scratch[3 * chunks :]
     nz, plane = n_row // 2, 2 * n_col
@@ -26,6 +29,10 @@
     hub_near = half - 1 + upper
     hub_far = half - upper
     is_hub = z == hub_near
+    orbital = z * plane + p
+    energy_ref[0] = eps_ref[orbital]
+    for t in range(rounds):
+        energy_ref[t + 1] = eps_ref[partner_ref[t, orbital]]
 
     def device(zz, q):
         return (zz * 2 + q // n_col, q % n_col)
@@ -162,16 +169,17 @@
         serve(k, 0, hub_near).wait_recv()
         send_back(k)
 
-    start_spread(0)
-    for s in range(chunks + 2):
-        if s + 1 < chunks:
-            start_spread(s + 1)
+    for k in range(min(AHEAD, chunks)):
+        start_spread(k)
+    for s in range(chunks + LEAF_LAG):
+        if s + AHEAD < chunks:
+            start_spread(s + AHEAD)
         if s < chunks:
             send_line(s)
-        if 1 <= s <= chunks:
-            pl.when(is_hub)(functools.partial(hub_step, s - 1))
-        if s >= 2:
-            pl.when(jnp.logical_not(is_hub))(functools.partial(leaf_step, s - 2))
+        if HUB_LAG <= s < chunks + HUB_LAG:
+            pl.when(is_hub)(functools.partial(hub_step, s - HUB_LAG))
+        if s >= LEAF_LAG:
+            pl.when(jnp.logical_not(is_hub))(functools.partial(leaf_step, s - LEAF_LAG))
 
     for k in range(chunks):
         for t in range(rounds):
@@ -190,20 +198,25 @@
                 serve(k, i, served(i)).wait_send()
 
 
-def exchange(n_row, n_col, partner, own):
+def exchange(n_row, n_col, partner, eps_occ, own):
     rounds = partner.shape[0]
     nz, plane = n_row // 2, 2 * n_col
     leaves = nz // 2 - 1
     chunks = CHUNKS
+    while chunks % 2 == 0 and chunks * plane * (2 + 2 * rounds) > SEMAPHORES:
+        chunks //= 2
     rows, width = own.shape[0] // 2 // chunks, own.shape[1] // n_col
     piece = (rows, width)
     dma = pltpu.SemaphoreType.DMA
     held = (nz + rounds * (leaves + 1)) * plane * rows * width * 4 * chunks
     return pl.pallas_call(
         functools.partial(exchange_kernel, n_row, n_col, rounds, chunks),
-        out_shape=jax.ShapeDtypeStruct((rounds,) + own.shape, jnp.float32),
-        in_specs=[pl.BlockSpec(memory_space=pltpu.SMEM), pl.BlockSpec(memory_space=pl.ANY)],
-        out_specs=pl.BlockSpec(memory_space=pl.ANY),
+        out_shape=(
+            jax.ShapeDtypeStruct((rounds,) + own.shape, jnp.float32),
+            jax.ShapeDtypeStruct((rounds + 1,), jnp.float32),
+        ),
+        in_specs=[pl.BlockSpec(memory_space=pltpu.SMEM)] * 2 + [pl.BlockSpec(memory_space=pl.ANY)],
+        out_specs=(pl.BlockSpec(memory_space=pl.ANY), pl.BlockSpec(memory_space=pltpu.SMEM)),
         scratch_shapes=[pltpu.VMEM((nz * plane,) + piece, jnp.float32)] * chunks
         + [pltpu.VMEM((rounds * plane,) + piece, jnp.float32)] * chunks
         + [pltpu.VMEM((leaves, rounds * plane) + piece, jnp.float32)] * chunks
@@ -223,10 +236,17 @@
             collective_id=0, has_side_effects=True, vmem_limit_bytes=held + 4 * 2**20
         ),
         name="exchange",
-    )(partner, own)
-
-
-def reduce_kernel(n_row, n_col, own_ref, out_ref, landed, total, final, as_, ar, bs, br):
+    )(partner, eps_occ, own)
+
+
+def two_parts(value):
+    high = value.astype(jnp.bfloat16)
+    return high, (value - high.astype(jnp.float32)).astype(jnp.bfloat16)
+
+
+def reduce_kernel(
+    n_row, n_col, own_ref, tamp_ref, mate_ref, out_ref, gamma_ref, landed, total, final, high, low, as_, ar, bs, br
+):
     nz, plane = n_row // 2, 2 * n_col
     row, col = lax.axis_index("row"), lax.axis_index("col")
     z, y = row // 2, row % 2
@@ -235,12 +255,12 @@
     def device(zz, q):
         return (zz * 2 + q // n_col, q % n_col)
 
-    def each(count, body):
+    def each(count, body, start=1):
         def step(i, carry):
             body(i)
             return carry
 
-        lax.fori_loop(1, count, step, 0)
+        lax.fori_loop(start, count, step, 0)
 
     def in_plane(o):
         q = lax.rem(p + o, plane)
@@ -277,6 +297,19 @@
     pl.semaphore_wait(barrier, plane - 1 + nz - 1)
     each(plane, lambda o: in_plane(o).start())
     total[...] = own_ref[p]
+    split = gamma_ref.shape[1] // COLUMNS
+    early = split * 3 // 4
+    high[...], low[...] = two_parts(tamp_ref[...])
+
+    def gamma_part(i):
+        columns = pl.ds(pl.multiple_of(i * COLUMNS, COLUMNS), COLUMNS)
+        mate_high, mate_low = two_parts(mate_ref[:, columns])
+        part = jnp.dot(low[...], mate_high, preferred_element_type=jnp.float32)
+        part += jnp.dot(high[...], mate_low, preferred_element_type=jnp.float32)
+        part += jnp.dot(high[...], mate_high, preferred_element_type=jnp.float32)
+        gamma_ref[:, columns] = part
+
+    each(early, gamma_part, 0)
 
     def add_plane(o):
         in_plane(o).wait_recv()
@@ -285,6 +318,7 @@
     each(plane, add_plane)
     each(nz, lambda o: in_line(o).start())
     final[0] = total[z]
+    each(split, gamma_part, early)
 
     def add_line(o):
         in_line(o).wait_recv()
@@ -296,54 +330,54 @@
     each(nz, lambda o: in_line(o).wait_send())
 
 
-def reduce_density(n_row, n_col, dens):
+def reduce_density(n_row, n_col, dens, tamps, stacked):
     nz, plane = n_row // 2, 2 * n_col
     tile = (dens.shape[0] // n_row, dens.shape[1] // n_col)
     pieces = dens.reshape(nz, 2, tile[0], n_col, tile[1]).transpose(1, 3, 0, 2, 4).reshape((plane, nz) + tile)
     dma = pltpu.SemaphoreType.DMA
     return pl.pallas_call(
         functools.partial(reduce_kernel, n_row, n_col),
-        out_shape=jax.ShapeDtypeStruct(tile, jnp.float32),
-        in_specs=[pl.BlockSpec(memory_space=pltpu.VMEM)],
-        out_specs=pl.BlockSpec(memory_space=pltpu.VMEM),
+        out_shape=(
+            jax.ShapeDtypeStruct(tile, jnp.float32),
+            jax.ShapeDtypeStruct((tamps.shape[0], stacked.shape[1]), jnp.float32),
+        ),
+        in_specs=[pl.BlockSpec(memory_space=pltpu.VMEM)] * 3,
+        out_specs=(pl.BlockSpec(memory_space=pltpu.VMEM),) * 2,
         scratch_shapes=[
             pltpu.VMEM((plane, nz) + tile, jnp.float32),
             pltpu.VMEM((nz,) + tile, jnp.float32),
             pltpu.VMEM((nz,) + tile, jnp.float32),
+            pltpu.VMEM(tamps.shape, jnp.bfloat16),
+            pltpu.VMEM(tamps.shape, jnp.bfloat16),
             dma((plane,)),
             dma((plane,)),
             dma((nz,)),
             dma((nz,)),
         ],
         compiler_params=pltpu.CompilerParams(
-            collective_id=1, has_side_effects=True, vmem_limit_bytes=16 * 2**20
+            collective_id=1, has_side_effects=True, vmem_limit_bytes=20 * 2**20
         ),
         name="reduce_density",
-    )(pieces)
+    )(pieces, tamps, stacked)
 
 
 def local(blocks, eps_occ, eps_vir, partner):
     own = blocks[0]
     n_row, n_col = lax.axis_size("row"), lax.axis_size("col")
-    orbital = lax.axis_index("row") * n_col + lax.axis_index("col")
-    energy_own = lax.dynamic_index_in_dim(eps_occ, orbital, 0, keepdims=False)
-    mates = exchange(n_row, n_col, partner, own)
+    mates, energies = exchange(n_row, n_col, partner, eps_occ, own)
     rounds = partner.shape[0]
     vir = own.shape[0]
     stacked = mates.reshape(rounds * vir, own.shape[1])
     pairs = jnp.dot(own, stacked.T, precision=DOT, preferred_element_type=jnp.float32)
     amps, tamps = [], []
     for t in range(rounds):
-        mate = lax.dynamic_index_in_dim(partner[t], orbital, 0, keepdims=False)
-        energy = lax.dynamic_index_in_dim(eps_occ, mate, 0, keepdims=False)
-        denom = eps_vir[:, None] + eps_vir[None, :] - energy_own - energy
+        denom = eps_vir[:, None] + eps_vir[None, :] - energies[0] - energies[t + 1]
         amp = -pairs[:, t * vir : (t + 1) * vir] / denom
         amps.append(amp)
         tamps.append(2.0 * amp - amp.T)
     amps, tamps = jnp.concatenate(amps, axis=1), jnp.concatenate(tamps, axis=1)
     dens = jnp.dot(amps, tamps.T, precision=DOT, preferred_element_type=jnp.float32)
-    tile = reduce_density(n_row, n_col, dens)
-    gamma = jnp.dot(tamps, stacked, precision=DOT, preferred_element_type=jnp.float32)
+    tile, gamma = reduce_density(n_row, n_col, dens, tamps, stacked)
     return gamma[None], tile
 
 

time: 222 us -> 208 us (0.937)
  matrix products: 15.7 us -> 5.16 us
  local copies, waits for them, and re-layouts: 6.88 us -> 11 us
  Pallas kernels: 192 us -> 188 us
  between operations: 4.62 us -> 0.77 us
    dot_general x1 -> x0, matrix products: 8.6 us -> none  [local(): jnp.dot(tamps, stacked, precision=DOT, preferred_element_type=jnp.float32)]
    unnamed x9 -> x16, local copies, waits for them, and re-layouts: 3.19 us -> 8.28 us
    pallas_call x1, Pallas kernels: 175 us -> 173 us  [exchange(): pl.pallas_call(functools.partial(exchange_kernel, n_row, n_col, rounds, c...]
where the time goes in v3:
time: 208 us; the launch traced here: 207 us
  Pallas kernels  188 us (90%)
  local copies, waits for them, and re-layouts  11 us (5%)
  matrix products  5.16 us (2%)
  other arithmetic  2.46 us (1%)
    pallas_call x1, Pallas kernels, exchange(): pl.pallas_call(functools.partial(exchange_kernel, n_row, n_col, rounds, c...  173 us
    pallas_call x1, Pallas kernels, reduce_density(): pl.pallas_call(functools.partial(reduce_kernel, n_row, n_col), out_shape=...  15.2 us
    unnamed x16, local copies, waits for them, and re-layouts  8.28 us

profile of v3, /device:TPU:0, one launch (start us, length us, event | category | flops | bytes accessed | tf_op | source)
XLA Modules:
  0.0 207.4 jit_solution(16701731672978780080)
XLA Ops:
  0.6 0.0 copy-start.2
  0.6 1.9 copy-done.2
  2.5 0.0 copy-start.4
  2.5 0.7 copy-done.4
  3.2 0.7 copy-done.5
  3.9 0.0 copy-start.3
  3.9 172.8 %exchange.1 = (f32[2,384,2048]{2,1,0:T(8,128)S(1)}, f32[3]{0:T(128)S(1)}) custom-call(s32[2,32]{1,0:T(2,128)S(1)} %copy-done.4, f32[32]{0:T(128)S(1)} %copy-done.5, f32[384,2048]{1,0:T(8,128)S(1)} %bitcast.20), custom_call_target="tpu_custom_call" | custom-call | tf_op jit(solution)/shard_map/exchange/pallas_call | solution.py:212
  176.7 0.0 copy-start
  176.7 0.8 fusion.8
  177.5 0.0 copy-done.3
  177.5 4.1 %convolution_bitcast_fusion = f32[384,768]{1,0:T(8,128)S(1)} fusion(f32[768,2048]{1,0:T(8,128)S(1)} %bitcast.18, f32[1,384,2048]{2,1,0:T(8,128)S(1)} %copy-done.3), kind=kOutput, calls=%fused_computation | convolution fusion | flops 3623878656 | bytes 10616832 | tf_op jit(solution)/shard_map/dot_general | solution.py:371
  181.6 0.0 copy-done
  181.6 0.0 copy-done.6
  181.6 2.2 %fusion.4 = (f32[384,384]{1,0:T(8,128)S(1)}, f32[384,384]{1,0:T(8,128)S(1)}, f32[384,384]{1,0:T(8,128)S(1)}) fusion(f32[384,768]{1,0:T(8,128)S(1)} %convolution_bitcast_fusion, f32[]{:T(128)} %bitcast.4, f32[]{:T(128)} %bitcast.3, f32[384]{0:T(512)S(1)} %copy-done.6, f32[]{:T(128)} %bitcast.5), kind=kLoop, calls=%fused_computation.8 | loop fusion | flops 1032192 | bytes 2953228 | tf_op jit(solution)/shard_map/div | solution.py:375
  183.7 0.2 copy.7
  184.0 0.2 copy.8
  184.2 0.1 broadcast_multiply_fusion
  184.3 0.2 copy.11
  184.5 0.1 bitcast_subtract_fusion
  184.6 0.2 copy.9
  184.8 0.2 copy.10
  185.1 0.1 bitcast_subtract_fusion.1
  185.1 0.2 copy.12
  185.4 1.1 fusion
  186.5 0.1 pad_maximum_fusion.tamp_ref
  186.6 0.5 reshape.16
  187.0 0.1 copy.13
  187.1 0.0 copy-start.1
  187.1 2.8 %copy-done.1 = f32[2,384,2048]{2,1,0:T(8,128)S(1)} copy-done((f32[2,384,2048]{2,1,0:T(8,128)S(1)}, f32[2,384,2048]{2,1,0:T(8,128)}, u32[]{:S(2)}) %copy-start.1) | copy-done | bytes 6291480
  189.9 15.2 %reduce_density.1 = (f32[48,96]{1,0:T(8,128)S(1)}, f32[384,2048]{1,0:T(8,128)S(1)}) custom-call(f32[8,4,48,96]{3,2,1,0:T(8,128)S(1)} %bitcast.22, f32[384,768]{1,0:T(8,128)S(1)} %pad_maximum_fusion.tamp_ref, f32[768,2048]{1,0:T(8,128)S(1)} %bitcast.19), custom_call_target="tpu_custom_call" | custom-call | tf_op jit(solution)/shard_map/reduce_density/pallas_call | solution.py:338
  205.1 1.7 copy.17
  206.8 0.6 copy.18
  (2 shorter events, 0.0 us)
Async XLA Ops:
  0.6 1.9 copy-start.2
  2.5 0.7 copy-start.4
  3.2 0.7 copy-start.5
  3.9 173.6 %copy-start.3 = (f32[1,384,2048]{2,1,0:T(8,128)S(1)}, f32[1,384,2048]{2,1,0:T(8,128)}, u32[]{:S(2)}) copy-start(f32[1,384,2048]{2,1,0:T(8,128)} %param.4) | copy-start | bytes 9437188
  176.7 4.9 %copy-start = (f32[2,384,2048]{2,1,0:T(8,128)}, f32[2,384,2048]{2,1,0:T(8,128)S(1)}, u32[]{:S(2)}) copy-start(f32[2,384,2048]{2,1,0:T(8,128)S(1)} %get-tuple-element.6) | copy-start | bytes 18874372
  177.5 4.1 %copy-start.6 = (f32[384]{0:T(512)S(1)}, f32[384]{0:T(512)}, u32[]{:S(2)}) copy-start(f32[384]{0:T(512)} %param.6) | copy-start | bytes 4612
  187.1 2.8 %copy-start.1 = (f32[2,384,2048]{2,1,0:T(8,128)S(1)}, f32[2,384,2048]{2,1,0:T(8,128)}, u32[]{:S(2)}) copy-start(f32[2,384,2048]{2,1,0:T(8,128)} %copy-done) | copy-start | bytes 18874372
